TPU v7x, 512 devices: a whole 4x4x16 slice. The times are simulated.
512 devices in a mesh: gx: 32 (over y_hi, z), gy: 4 (over x), gz: 4 (over y_lo, core).
Axes of the slice: x: 4, y: 4 (y_hi: 2, y_lo: 2; y = y_hi * 2 + y_lo), z: 16, core: 2. Of those that a mesh axis runs over, the one named last changes fastest.
Arguments:
- fields: float32 [12, 256, 32, 512], P(None, 'gx', 'gy', 'gz'), as said below
- reacting: int32 [256, 32, 512], P('gx', 'gy', 'gz'), may hold values from 0 to 1, as said below
- panel_map: int32 [2, 256, 512], P(None, 'gx', 'gz'), may hold values from 0 to 4095, as said below
- layer_one: bfloat16 [1600, 12], replicated, may hold values from -4 to 4
- layer_two: bfloat16 [800, 1600], replicated, may hold values from -0.21875 to 0.21875
- layer_three: bfloat16 [400, 800], replicated, may hold values from -0.3125 to 0.3125
- layer_four: bfloat16 [12, 400], replicated, may hold values from -0.3125 to 0.3125
Outputs:
- new_fields: float32 [12, 256, 32, 512], P(None, 'gx', 'gy', 'gz')
- impulse: float32 [4096], P(('gx', 'gy', 'gz'))
Inputs may be any that keep to these rules, and one draw needn't show every extreme that they name: `fields`: component 0 (density) lies between 0.3 and 3.3; the velocities (components 1 to 3 over component 0) between -1.2 and 1.2; the pressure 0.4 (component 4 - |momentum|^2 / (2 density)) between 0.3 and 5; components 5 to 11 are 0.01 to 0.14 times component 0. Each device's aligned block of 8 x 8 x 128 cells holds at most 256 reacting cells. The blocks that share their ranges along the second and third dimensions hold exactly 64 reacting cells each on average, and one in eight of them, and at least one, hold exactly 256. `panel_map`: every panel is a patch of 8 x 8 cells of one wall, shifted by 4 cells along the first dimension and closed around it; panels are numbered in a random order and each number is used once.
All inputs are finite; a program needn't handle non-finite values.
Results may differ from a plain program's by a relative error of at most 0.0014.
Values may be sent and summed in bfloat16 or wider, within the bound.
A program may use at most 64 MiB of HBM per device.

v0:
```python
import jax
import jax.numpy as jnp
from jax import lax
from jax.sharding import PartitionSpec as P

BAL = 64
COMPS = 12
PATCH = 8
HEAT_RATIO = 1.4
TIME_STEP = 0.1
CHEM_STEP = 0.25
WENO_EPS = 1e-06


def extended(array, sides, width):
    for axis, dim in sides:
        size, length = (lax.axis_size(axis), array.shape[dim])
        up = [(i, (i + 1) % size) for i in range(size - 1)]
        down = [(j, i) for i, j in up]
        last = lax.slice_in_dim(array, length - width, length, axis=dim)
        initial = lax.slice_in_dim(array, 0, width, axis=dim)
        before = lax.ppermute(last, axis, up)
        after = lax.ppermute(initial, axis, down)
        array = jnp.concatenate([before, array, after], axis=dim)
    return array


def take_slab(array_in, begin_at, length_of, flux_axis):
    return lax.slice_in_dim(array_in, begin_at, begin_at + length_of, axis=flux_axis)


def weno_face(upwind_two, upwind_one, center, downwind_one, downwind_two):
    cand_zero = (2.0 * upwind_two - 7.0 * upwind_one + 11.0 * center) / 6.0
    cand_one = (-upwind_one + 5.0 * center + 2.0 * downwind_one) / 6.0
    cand_two = (2.0 * center + 5.0 * downwind_one - downwind_two) / 6.0
    smooth_zero = (
        13.0 / 12.0 * (upwind_two - 2.0 * upwind_one + center) ** 2
        + 0.25 * (upwind_two - 4.0 * upwind_one + 3.0 * center) ** 2
    )
    smooth_one = (
        13.0 / 12.0 * (upwind_one - 2.0 * center + downwind_one) ** 2
        + 0.25 * (upwind_one - downwind_one) ** 2
    )
    smooth_two = (
        13.0 / 12.0 * (center - 2.0 * downwind_one + downwind_two) ** 2
        + 0.25 * (3.0 * center - 4.0 * downwind_one + downwind_two) ** 2
    )
    weight_zero = 0.1 / (WENO_EPS + smooth_zero) ** 2
    weight_one = 0.6 / (WENO_EPS + smooth_one) ** 2
    weight_two = 0.3 / (WENO_EPS + smooth_two) ** 2
    weight_sum = weight_zero + weight_one + weight_two
    return (weight_zero * cand_zero + weight_one * cand_one + weight_two * cand_two) / weight_sum


def to_recon(fields):
    density = fields[0]
    velocity = fields[1:4] / density[None]
    pressure = (HEAT_RATIO - 1.0) * (
        fields[4] - 0.5 * density * jnp.sum(velocity * velocity, axis=0)
    )
    fractions = fields[5:] / density[None]
    return jnp.concatenate(
        [jnp.log(density)[None], velocity, jnp.log(pressure)[None], fractions], axis=0
    )


def normal_of(normal, ndims):
    return (jnp.arange(3) == normal).reshape((3,) + (1,) * (ndims - 1))


def side_terms(recon, normal):
    density = jnp.exp(recon[0])
    velocity = recon[1:4]
    pressure = jnp.exp(recon[4])
    fractions = recon[5:]
    speed_n = velocity[normal]
    energy = pressure / (HEAT_RATIO - 1.0) + 0.5 * density * jnp.sum(velocity * velocity, axis=0)
    conserved = jnp.concatenate(
        [density[None], density[None] * velocity, energy[None], density[None] * fractions], axis=0
    )
    mass_flux = density * speed_n
    normal_mask = normal_of(normal, recon.ndim)
    momentum_flux = mass_flux[None] * velocity + jnp.where(normal_mask, pressure[None], 0.0)
    flux_terms = jnp.concatenate(
        [
            mass_flux[None],
            momentum_flux,
            ((energy + pressure) * speed_n)[None],
            mass_flux[None] * fractions,
        ],
        axis=0,
    )
    sound_speed = jnp.sqrt(HEAT_RATIO * pressure / density)
    return (
        density,
        velocity,
        pressure,
        fractions,
        energy,
        conserved,
        flux_terms,
        speed_n,
        sound_speed,
    )


def star_state(
    density, velocity, pressure, fractions, energy, speed_n, wave_speed, contact, normal_mask
):
    relative = wave_speed - speed_n
    factor = density * relative / (wave_speed - contact)
    star_velocity = jnp.where(normal_mask, contact[None], velocity)
    star_energy = energy / density + (contact - speed_n) * (
        contact + pressure / (density * relative)
    )
    return jnp.concatenate(
        [
            factor[None],
            factor[None] * star_velocity,
            (factor * star_energy)[None],
            factor[None] * fractions,
        ],
        axis=0,
    )


def hllc_flux(left_recon, right_recon, normal):
    (
        left_density,
        left_velocity,
        left_pressure,
        left_fractions,
        left_energy,
        left_cons,
        left_flux,
        left_speed,
        left_sound,
    ) = side_terms(left_recon, normal)
    (
        right_density,
        right_velocity,
        right_pressure,
        right_fractions,
        right_energy,
        right_cons,
        right_flux,
        right_speed,
        right_sound,
    ) = side_terms(right_recon, normal)
    wave_left = jnp.minimum(left_speed - left_sound, right_speed - right_sound)
    wave_right = jnp.maximum(left_speed + left_sound, right_speed + right_sound)
    left_rel = wave_left - left_speed
    right_rel = wave_right - right_speed
    contact = (
        right_pressure
        - left_pressure
        + left_density * left_speed * left_rel
        - right_density * right_speed * right_rel
    ) / (left_density * left_rel - right_density * right_rel)
    normal_mask = normal_of(normal, left_recon.ndim)
    star_left = star_state(
        left_density,
        left_velocity,
        left_pressure,
        left_fractions,
        left_energy,
        left_speed,
        wave_left,
        contact,
        normal_mask,
    )
    star_right = star_state(
        right_density,
        right_velocity,
        right_pressure,
        right_fractions,
        right_energy,
        right_speed,
        wave_right,
        contact,
        normal_mask,
    )
    left_star_flux = left_flux + wave_left[None] * (star_left - left_cons)
    right_star_flux = right_flux + wave_right[None] * (star_right - right_cons)
    return jnp.where(
        wave_left[None] >= 0,
        left_flux,
        jnp.where(
            contact[None] >= 0,
            left_star_flux,
            jnp.where(wave_right[None] > 0, right_star_flux, right_flux),
        ),
    )


def face_flux(padded, normal):
    flux_axis = normal + 1
    face_count = padded.shape[flux_axis] - 5
    stencil = [take_slab(padded, offset, face_count, flux_axis) for offset in range(6)]
    left_state = weno_face(stencil[0], stencil[1], stencil[2], stencil[3], stencil[4])
    right_state = weno_face(stencil[5], stencil[4], stencil[3], stencil[2], stencil[1])
    return hllc_flux(left_state, right_state, normal)


def mirror_walls(padded, normal, at_first, at_last):
    flux_axis = normal + 1
    cell_count = padded.shape[flux_axis] - 6
    flip_sign = (
        jnp.where(jnp.arange(padded.shape[0]) == 1 + normal, -1.0, 1.0)
        .astype(padded.dtype)
        .reshape((-1, 1, 1, 1))
    )
    ghost_low = jnp.flip(take_slab(padded, 3, 3, flux_axis), flux_axis) * flip_sign
    ghost_high = jnp.flip(take_slab(padded, cell_count, 3, flux_axis), flux_axis) * flip_sign
    low_side = jnp.where(at_first, ghost_low, take_slab(padded, 0, 3, flux_axis))
    high_side = jnp.where(at_last, ghost_high, take_slab(padded, cell_count + 3, 3, flux_axis))
    return jnp.concatenate(
        [low_side, take_slab(padded, 3, cell_count, flux_axis), high_side], axis=flux_axis
    )


def chem_rates(features, layer_one, layer_two, layer_three, layer_four):
    hidden_one = jax.nn.gelu(
        jnp.dot(layer_one, features, preferred_element_type=jnp.float32)
    ).astype(jnp.bfloat16)
    hidden_two = jax.nn.gelu(
        jnp.dot(layer_two, hidden_one, preferred_element_type=jnp.float32)
    ).astype(jnp.bfloat16)
    hidden_three = jax.nn.gelu(
        jnp.dot(layer_three, hidden_two, preferred_element_type=jnp.float32)
    ).astype(jnp.bfloat16)
    return jnp.dot(layer_four, hidden_three, preferred_element_type=jnp.float32).astype(
        jnp.bfloat16
    )


def body(fields, reacting, panel_map, layer_one, layer_two, layer_three, layer_four):
    recon_fields = to_recon(fields)
    gx_count = lax.axis_size("gx")
    gy_count = lax.axis_size("gy")
    gz_count = lax.axis_size("gz")
    at_first = (lax.axis_index("gx") == 0, lax.axis_index("gy") == 0, lax.axis_index("gz") == 0)
    at_last = (
        lax.axis_index("gx") == gx_count - 1,
        lax.axis_index("gy") == gy_count - 1,
        lax.axis_index("gz") == gz_count - 1,
    )
    padded = extended(recon_fields, (("gx", 1), ("gy", 2), ("gz", 3)), 3)
    line_fields = (padded[:, :, 3:-3, 3:-3], padded[:, 3:-3, :, 3:-3], padded[:, 3:-3, 3:-3, :])
    update = jnp.zeros_like(fields)
    push_low = None
    push_high = None
    for normal in range(3):
        line_block = mirror_walls(line_fields[normal], normal, at_first[normal], at_last[normal])
        face_fluxes = face_flux(line_block, normal)
        cell_count = face_fluxes.shape[normal + 1] - 1
        change = take_slab(face_fluxes, 1, cell_count, normal + 1) - take_slab(
            face_fluxes, 0, cell_count, normal + 1
        )
        update = update + change
        if normal == 1:
            push_low = face_fluxes[2, :, 0, :]
            push_high = face_fluxes[2, :, cell_count, :]
    cell_total = reacting.size
    react_flags = reacting.reshape(cell_total)
    capacity = BAL * min(4, gx_count)
    per_peer = capacity // gx_count
    row_rank = jnp.cumsum(react_flags) - 1
    slot_index = jnp.where(
        react_flags == 1, row_rank % gx_count * per_peer + row_rank // gx_count, capacity
    )
    flat_features = recon_fields.reshape(COMPS, cell_total).astype(jnp.bfloat16)
    packed = (
        jnp.zeros((COMPS, capacity), jnp.bfloat16).at[:, slot_index].set(flat_features, mode="drop")
    )
    rate_packed = chem_rates(packed, layer_one, layer_two, layer_three, layer_four)
    gathered = rate_packed[:, jnp.where(react_flags == 1, slot_index, 0)]
    source = jnp.where(react_flags[None, :] == 1, gathered.astype(jnp.float32), 0.0).reshape(
        fields.shape
    )
    new_fields = fields - TIME_STEP * update + CHEM_STEP * source
    on_low = lax.axis_index("gy") == 0
    on_high = lax.axis_index("gy") == gy_count - 1
    push_values = jnp.concatenate(
        [
            jnp.where(on_low, push_low, 0.0).reshape(-1),
            jnp.where(on_high, push_high, 0.0).reshape(-1),
        ]
    )
    panel_ids = jnp.concatenate([panel_map[0].reshape(-1), panel_map[1].reshape(-1)])
    panels_all = 2 * (fields.shape[1] * gx_count // PATCH) * (fields.shape[3] * gz_count // PATCH)
    own_panels = panels_all // (gx_count * gy_count * gz_count)
    partial_loads = jax.ops.segment_sum(push_values, panel_ids, num_segments=panels_all)
    totals = lax.psum(partial_loads, ("gx", "gy", "gz"))
    flat_index = (
        lax.axis_index("gx") * gy_count + lax.axis_index("gy")
    ) * gz_count + lax.axis_index("gz")
    result = lax.dynamic_slice_in_dim(totals, flat_index * own_panels, own_panels)
    impulse = result / float(PATCH * PATCH)
    return (new_fields, impulse)


def solution(mesh):
    return jax.shard_map(
        body,
        mesh=mesh,
        in_specs=(
            P(None, "gx", "gy", "gz"),
            P("gx", "gy", "gz"),
            P(None, "gx", "gz"),
            P(),
            P(),
            P(),
            P(),
        ),
        out_specs=(P(None, "gx", "gy", "gz"), P(("gx", "gy", "gz"))),
        check_vma=False,
    )
```

profile of v0, /device:TPU:1, one launch (start us, length us, event | category | flops | bytes accessed | tf_op | source)
XLA Modules:
  0.0 275.4 jit_solution(14904916895954684997)
XLA Ops:
  0.6 0.9 convert_bitcast_fusion.3
  1.6 0.9 convert_bitcast_fusion.1
  2.5 1.0 convert_bitcast_fusion
  3.5 0.8 convert_bitcast_fusion.2
  4.3 0.8 fusion.173
  5.1 5.0 %collective-permute-start = (f32[12,3,8,128]{3,2,1,0:T(8,128)}, f32[12,3,8,128]{3,2,1,0:T(8,128)}, u32[]{:S(2)}, u32[]{:S(2)}) collective-permute-start(f32[12,3,8,128]{3,2,1,0:T(8,128)} %get-tuple-element.138), channel_id=1, source_target_pairs={{0,16},{16,32},{32,48},{48,64},{64,80},{80,96},{96,112},{112,128},... | collective-permute-start | bytes 442376 | tf_op jit(solution)/shard_map/ppermute | solution.py:22
  10.2 1.3 collective-permute-start.1
  11.4 0.9 fusion.171
  12.3 0.5 iota_compare_fusion.1
  12.8 0.5 compare_select_fusion.7
  13.3 0.6 iota_compare_fusion.2
  13.9 0.9 fusion.172
  14.8 0.5 compare_select_fusion.5
  15.5 0.9 maximum_bitcast_fusion
  16.4 2.7 copy.63
  19.4 0.7 slice.440
  20.1 0.9 reduce-window.12
  21.6 21.7 %scatter_custom_fusion = bf16[12,256]{0,1:T(8,128)(2,1)} fusion(s32[8192]{0:T(1024)S(1)} %bitcast.214, bf16[8192,12]{1,0:T(8,128)(2,1)} %copy.63, bf16[]{:T(256)} %constant.78.clone.1), kind=kCustom, calls=%fused_computation.316 | custom fusion | bytes 6656 | tf_op jit(solution)/shard_map/scatter | solution.py:274
  43.3 3.2 %fusion.16 = bf16[800,256]{1,0:T(8,128)(2,1)} fusion(bf16[800,1600]{1,0:T(8,128)(2,1)S(1)} %copy-done, bf16[12,256]{0,1:T(8,128)(2,1)} %scatter_custom_fusion, bf16[1600,12]{0,1:T(8,128)(2,1)} %param.10), kind=kOutput, calls=%fused_computation.28 | convolution fusion | flops 670720000 | bytes 3014144 | tf_op jit(solution)/shard_map/dot_general | solution.py:227
  46.5 1.8 fusion.8
  48.2 0.6 iota_compare_fusion
  48.8 1.8 rev.23
  50.6 1.8 rev.24
  52.4 1.9 rev.25
  54.3 0.9 rev.26
  55.4 29.4 %gather_fusion = bf16[8192,12]{1,0:T(8,128)(2,1)} fusion(bf16[12,256]{0,1:T(8,128)(2,1)S(1)} %copy.64, s32[8192]{0:T(1024)S(1)} %broadcast_clamp_fusion), kind=kCustom, calls=%fused_computation | custom fusion | bytes 425984 | tf_op jit(solution)/shard_map/gather | solution.py:277
  84.8 3.8 %convert_element_type.31 = f32[8192,12]{1,0:T(8,128)} convert(bf16[8192,12]{1,0:T(8,128)(2,1)} %gather_fusion) | non-fusion elementwise | flops 98304 | bytes 589824 | tf_op jit(solution)/shard_map/convert_element_type | solution.py:278
  88.6 3.6 %copy.66 = f32[12,8,8,128]{3,2,1,0:T(8,128)} copy(f32[12,8,8,128]{0,3,2,1:T(8,128)} %bitcast.175) | data formatting | bytes 786432 | tf_op jit(solution)/shard_map/convert_element_type | solution.py:278
  92.1 0.6 pad_add_fusion
  92.8 1.2 multiply_select_fusion.2
  94.0 1.9 add_divide_fusion.2
  96.0 1.0 pad_maximum_fusion.5
  97.2 3.1 %collective-permute-start.2 = (f32[12,14,3,128]{3,1,2,0:T(8,128)S(1)}, f32[12,14,3,128]{3,1,2,0:T(8,128)S(1)}, u32[]{:S(2)}, u32[]{:S(2)}) collective-permute-start(f32[12,14,3,128]{3,1,2,0:T(8,128)S(1)} %copy.53), channel_id=1, source_target_pairs={{0,4},{4,8},{8,12},{1,5},{5,9},{9,13},{2,6},{6,10},{10,14},{3,7},{... | collective-permute-start | bytes 774152 | tf_op jit(solution)/shard_map/ppermute | solution.py:22
  100.4 1.5 collective-permute-start.3
  102.2 0.4 copy-done.14
  103.0 1.9 collective-permute-done.2
  105.1 3.7 %collective-permute-done.3 = f32[12,14,3,128]{3,1,2,0:T(8,128)S(1)} collective-permute-done((f32[12,14,3,128]{3,1,2,0:T(8,128)S(1)}, f32[12,14,3,128]{3,1,2,0:T(8,128)S(1)}, u32[]{:S(2)}, u32[]{:S(2)}) %collective-permute-start.3) | collective-permute-done | bytes 258080 | tf_op jit(solution)/shard_map/ppermute | solution.py:23
  109.1 0.5 copy-done.4
  109.9 3.6 %add_divide_fusion.1 = (f32[12,8,9,128]{3,2,1,0:T(8,128)S(1)}, f32[12,8,9,128]{3,2,1,0:T(8,128)S(1)}) fusion(f32[12,8,11,128]{3,2,1,0:T(8,128)S(1)} %get-tuple-element.130, f32[12,8,11,128]{3,2,1,0:T(8,128)S(1)} %get-tuple-element.131), kind=kLoop, calls=%fused_computation.80 | loop fusion | flops 13713408 | bytes 3538944 | tf_op jit(solution)/shard_map/div | solution.py:52
  114.0 0.3 slice_multiply_fusion.6
  114.3 0.3 copy-done.13
  114.8 0.5 fusion.22
  115.4 0.9 copy-done.1
  116.2 14.0 %scatter_custom_fusion.1 = f32[4096]{0:T(1024)S(1)} fusion(s32[2048]{0:T(1024)} %pad_add_fusion, f32[2048]{0:T(1024)S(1)} %pad_maximum_fusion.9, f32[]{:T(128)} %constant.54.clone.1), kind=kCustom, calls=%fused_computation.342 | custom fusion | flops 2048 | bytes 16896 | tf_op jit(solution)/shard_map/scatter-add | solution.py:293
  130.3 111.0 %psum.7 = f32[4096]{0:T(1024)S(1)} all-reduce(f32[4096]{0:T(1024)S(1)} %scatter_custom_fusion.1), channel_id=1, replica_groups=mesh['gx'=32,'gy'=4,'gz'=4] {'gx','gy','gz'}, use_global_device_ids=true, to_apply=%region_11.12 | all-reduce | flops 4096 | bytes 32768 | tf_op jit(solution)/shard_map/psum | solution.py:294
  241.3 1.5 pad_maximum_fusion
  242.8 2.0 fusion.169
  244.8 3.4 %copy.59 = f32[12,14,14,3]{2,1,3,0:T(8,128)} copy(f32[12,14,14,3]{3,2,1,0:T(8,128)} %get-tuple-element.58) | data formatting | bytes 56448 | tf_op jit(solution)/shard_map/slice | solution.py:20
  248.2 2.1 collective-permute-start.4
  250.3 3.4 %copy.61 = f32[12,14,14,3]{2,1,3,0:T(8,128)} copy(f32[12,14,14,3]{3,2,1,0:T(8,128)} %get-tuple-element.57) | data formatting | bytes 56448 | tf_op jit(solution)/shard_map/slice | solution.py:21
  253.7 2.9 %collective-permute-start.5 = (f32[12,14,14,3]{2,1,3,0:T(8,128)}, f32[12,14,14,3]{2,1,3,0:T(8,128)}, u32[]{:S(2)}, u32[]{:S(2)}) collective-permute-start(f32[12,14,14,3]{2,1,3,0:T(8,128)} %copy.61), channel_id=1, source_target_pairs={{1,0},{2,1},{3,2},{5,4},{6,5},{7,6},{9,8},{10,9},{11,10},{13,12},{... | collective-permute-start | bytes 84680 | tf_op jit(solution)/shard_map/ppermute | solution.py:23
  256.6 0.6 dynamic-slice_multiply_fusion
  257.2 1.7 slice.418
  258.9 2.3 copy.67
  261.2 0.9 collective-permute-done.5
  262.1 1.7 slice.424
  263.8 2.3 copy.68
  266.1 1.5 multiply_select_fusion
  267.8 3.9 %add_divide_fusion = (f32[12,8,8,129]{3,2,1,0:T(8,128)S(1)}, f32[12,8,8,129]{3,2,1,0:T(8,128)S(1)}) fusion(f32[12,8,8,131]{3,2,1,0:T(8,128)S(1)} %get-tuple-element.134, f32[12,8,8,131]{3,2,1,0:T(8,128)S(1)} %get-tuple-element.135), kind=kLoop, calls=%fused_computation.53 | loop fusion | flops 12284928 | bytes 3170304 | tf_op jit(solution)/shard_map/div | solution.py:52
  272.3 0.3 slice_multiply_fusion
  272.6 0.3 copy-done.11
  273.1 0.5 fusion.24
  273.7 0.6 copy-done.2
  274.4 1.0 fusion.113
  (87 shorter events, 4.6 us)
Async XLA Ops:
  0.6 42.6 %copy-start = (bf16[800,1600]{1,0:T(8,128)(2,1)S(1)}, bf16[800,1600]{1,0:T(8,128)(2,1)}, u32[]{:S(2)}) copy-start(bf16[800,1600]{1,0:T(8,128)(2,1)} %param.11) | copy-start | bytes 7680004
  4.3 11.0 %copy-start.10 = (s32[2,8,128]{2,1,0:T(8,128)S(1)}, s32[2,8,128]{2,1,0:T(8,128)}, u32[]{:S(2)}) copy-start(s32[2,8,128]{2,1,0:T(8,128)} %param.9) | copy-start | bytes 24580
  5.1 87.6 %collective-permute-start = (f32[12,3,8,128]{3,2,1,0:T(8,128)}, f32[12,3,8,128]{3,2,1,0:T(8,128)}, u32[]{:S(2)}, u32[]{:S(2)}) collective-permute-start(f32[12,3,8,128]{3,2,1,0:T(8,128)} %get-tuple-element.138), channel_id=1, source_target_pairs={{0,16},{16,32},{32,48},{48,64},{64,80},{80,96},{96,112},{112,128},... | collective-permute-start | bytes 442376 | tf_op jit(solution)/shard_map/ppermute | solution.py:22
  10.2 82.6 %collective-permute-start.1 = (f32[12,3,8,128]{3,2,1,0:T(8,128)}, f32[12,3,8,128]{3,2,1,0:T(8,128)}, u32[]{:S(2)}, u32[]{:S(2)}) collective-permute-start(f32[12,3,8,128]{3,2,1,0:T(8,128)} %get-tuple-element.139), channel_id=1, source_target_pairs={{16,0},{32,16},{48,32},{64,48},{80,64},{96,80},{112,96},{128,112},... | collective-permute-start | bytes 442376 | tf_op jit(solution)/shard_map/ppermute | solution.py:23
  15.3 3.8 %copy-start.9 = (s32[8,8,128]{2,1,0:T(8,128)S(1)}, s32[8,8,128]{2,1,0:T(8,128)}, u32[]{:S(2)}) copy-start(s32[8,8,128]{2,1,0:T(8,128)} %param.8) | copy-start | bytes 98308
  43.3 3.2 %copy-start.16 = (bf16[12,400]{1,0:T(8,128)(2,1)S(1)}, bf16[12,400]{1,0:T(8,128)(2,1)}, u32[]{:S(2)}) copy-start(bf16[12,400]{1,0:T(8,128)(2,1)} %param.13) | copy-start | bytes 28804
  88.6 4.2 %copy-start.15 = (f32[12]{0:T(128)S(1)}, f32[12]{0:T(128)}, u32[]{:S(2)}) copy-start(f32[12]{0:T(128)} %compare_select_fusion.7) | copy-start | bytes 148
  97.2 7.7 %collective-permute-start.2 = (f32[12,14,3,128]{3,1,2,0:T(8,128)S(1)}, f32[12,14,3,128]{3,1,2,0:T(8,128)S(1)}, u32[]{:S(2)}, u32[]{:S(2)}) collective-permute-start(f32[12,14,3,128]{3,1,2,0:T(8,128)S(1)} %copy.53), channel_id=1, source_target_pairs={{0,4},{4,8},{8,12},{1,5},{5,9},{9,13},{2,6},{6,10},{10,14},{3,7},{... | collective-permute-start | bytes 774152 | tf_op jit(solution)/shard_map/ppermute | solution.py:22
  100.4 8.4 %collective-permute-start.3 = (f32[12,14,3,128]{3,1,2,0:T(8,128)S(1)}, f32[12,14,3,128]{3,1,2,0:T(8,128)S(1)}, u32[]{:S(2)}, u32[]{:S(2)}) collective-permute-start(f32[12,14,3,128]{3,1,2,0:T(8,128)S(1)} %copy.55), channel_id=1, source_target_pairs={{4,0},{8,4},{12,8},{5,1},{9,5},{13,9},{6,2},{10,6},{14,10},{7,3},{... | collective-permute-start | bytes 774152 | tf_op jit(solution)/shard_map/ppermute | solution.py:23
  102.0 0.7 copy-start.14
  102.7 6.2 %copy-start.7 = (f32[12,8,3,128]{3,2,1,0:T(4,128)S(1)}, f32[12,8,3,128]{3,2,1,0:T(4,128)}, u32[]{:S(2)}) copy-start(f32[12,8,3,128]{3,2,1,0:T(4,128)} %rev.23) | copy-start | bytes 442372
  102.7 6.2 %copy-start.8 = (f32[12,8,3,128]{3,2,1,0:T(4,128)S(1)}, f32[12,8,3,128]{3,2,1,0:T(4,128)}, u32[]{:S(2)}) copy-start(f32[12,8,3,128]{3,2,1,0:T(4,128)} %rev.24) | copy-start | bytes 442372
  105.0 4.1 %copy-start.3 = (f32[12,14,3,128]{3,2,1,0:T(4,128)}, f32[12,14,3,128]{3,2,1,0:T(4,128)S(1)}, u32[]{:S(2)}) copy-start(f32[12,14,3,128]{3,2,1,0:T(4,128)S(1)} %copy.54) | copy-start | bytes 774148
  109.0 0.7 copy-start.4
  114.0 0.7 copy-start.13
  115.3 0.9 copy-start.1
  248.2 9.0 %collective-permute-start.4 = (f32[12,14,14,3]{2,1,3,0:T(8,128)}, f32[12,14,14,3]{2,1,3,0:T(8,128)}, u32[]{:S(2)}, u32[]{:S(2)}) collective-permute-start(f32[12,14,14,3]{2,1,3,0:T(8,128)} %copy.59), channel_id=1, source_target_pairs={{0,1},{1,2},{2,3},{4,5},{5,6},{6,7},{8,9},{9,10},{10,11},{12,13},{... | collective-permute-start | bytes 84680 | tf_op jit(solution)/shard_map/ppermute | solution.py:22
  250.3 15.7 %copy-start.12 = (f32[12]{0:T(128)S(1)}, f32[12]{0:T(128)}, u32[]{:S(2)}) copy-start(f32[12]{0:T(128)} %compare_select_fusion.5) | copy-start | bytes 148
  253.7 8.3 %collective-permute-start.5 = (f32[12,14,14,3]{2,1,3,0:T(8,128)}, f32[12,14,14,3]{2,1,3,0:T(8,128)}, u32[]{:S(2)}, u32[]{:S(2)}) collective-permute-start(f32[12,14,14,3]{2,1,3,0:T(8,128)} %copy.61), channel_id=1, source_target_pairs={{1,0},{2,1},{3,2},{5,4},{6,5},{7,6},{9,8},{10,9},{11,10},{13,12},{... | collective-permute-start | bytes 84680 | tf_op jit(solution)/shard_map/ppermute | solution.py:23
  272.3 0.7 copy-start.11
  273.1 1.1 copy-start.2
  273.1 1.2 copy-start.5
  273.1 1.3 copy-start.6
where the time goes:
time: 276 us; the launch traced here: 275 us
  blocking collectives  111 us (40%)
  local copies, waits for them, and re-layouts  87.9 us (32%)
  other arithmetic  47.9 us (17%)
  starting transfers between devices  15.9 us (6%)
  waiting for transfers between devices  6.54 us (2%)
  matrix products  4.97 us (2%)
    psum x1, blocking collectives, body(): totals = lax.psum(partial_loads, ('gx', 'gy', 'gz'))  111 us
    gather x1, local copies, waits for them, and re-layouts, body(): gathered = rate_packed[:, jnp.where(react_flags == 1, slot_index, 0)]  29.4 us
    scatter x1, local copies, waits for them, and re-layouts, body(): jnp.zeros((COMPS, capacity), jnp.bfloat16).at[:, slot_index]  21.7 us
    scatter-add x1, other arithmetic, body(): jax.ops.segment_sum(push_values, panel_ids, num_segments=panels_all)  14 us
    ppermute x3, starting transfers between devices, extended(): before = lax.ppermute(last, axis, up)  10.3 us
    div x3, other arithmetic, weno_face(): (weight_zero * cand_zero + weight_one * cand_one + weight_two * cand_two)...  9.43 us
    unnamed x38, local copies, waits for them, and re-layouts  7.97 us
    ppermute x3, starting transfers between devices, extended(): after = lax.ppermute(initial, axis, down)  5.61 us
  transfers between devices with their start and end apart: 6, of which 3 were waited for; matrix products, arithmetic and copies ran while one was open for 33% of the time, Pallas kernels for 0%

commit v1 on v0

--- a/solution.py
+++ b/solution.py
@@ -291,7 +291,7 @@
     panels_all = 2 * (fields.shape[1] * gx_count // PATCH) * (fields.shape[3] * gz_count // PATCH)
     own_panels = panels_all // (gx_count * gy_count * gz_count)
     partial_loads = jax.ops.segment_sum(push_values, panel_ids, num_segments=panels_all)
-    totals = lax.psum(partial_loads, ("gx", "gy", "gz"))
+    totals = lax.all_gather(partial_loads, axis_name=("gx", "gy", "gz")).sum(axis=0)
     flat_index = (
         lax.axis_index("gx") * gy_count + lax.axis_index("gy")
     ) * gz_count + lax.axis_index("gz")

time: 276 us -> 914 us (3.31)
  waiting for transfers between devices: 6.54 us -> 722 us
  blocking collectives: 111 us -> 0 us
  between operations: 1.23 us -> 14.8 us
    all_gather x0 -> x1, waiting for transfers between devices: none -> 721 us  [body(): lax.all_gather(partial_loads, axis_name=('gx', 'gy', 'gz')).sum(axis=0)]
    psum x1 -> x0, blocking collectives: 111 us -> none  [body(): totals = lax.psum(partial_loads, ('gx', 'gy', 'gz'))]
    all_gather x0 -> x1, local copies, waits for them, and re-layouts: none -> 9.36 us  [body(): lax.all_gather(partial_loads, axis_name=('gx', 'gy', 'gz')).sum(axis=0)]
  transfers between devices with their start and end apart: 6 -> 7, of which waited for: 3 -> 3; matrix products, arithmetic and copies ran while one was open for 33% -> 11% of each run, Pallas kernels for 0% -> 0%
where the time goes in v1:
time: 914 us; the launch traced here: 908 us
  waiting for transfers between devices  722 us (79%)
  local copies, waits for them, and re-layouts  90.7 us (10%)
  other arithmetic  52.3 us (6%)
  starting transfers between devices  23.4 us (3%)
  between operations  14.8 us (2%)
    all_gather x1, waiting for transfers between devices, body(): lax.all_gather(partial_loads, axis_name=('gx', 'gy', 'gz')).sum(axis=0)  721 us
    gather x1, local copies, waits for them, and re-layouts, body(): gathered = rate_packed[:, jnp.where(react_flags == 1, slot_index, 0)]  24 us
    scatter x1, local copies, waits for them, and re-layouts, body(): jnp.zeros((COMPS, capacity), jnp.bfloat16).at[:, slot_index]  21.7 us
  transfers between devices with their start and end apart: 7, of which 3 were waited for; matrix products, arithmetic and copies ran while one was open for 11% of the time, Pallas kernels for 0%

profile of v1, /device:TPU:1, one launch (start us, length us, event | category | flops | bytes accessed | tf_op | source)
XLA Modules:
  0.0 908.0 jit_solution(2373488764508664838)
XLA Ops:
  7.2 1.5 convert_bitcast_fusion.3
  8.8 1.6 convert_bitcast_fusion
  10.4 0.9 convert_bitcast_fusion.1
  11.3 1.4 convert_bitcast_fusion.2
  12.8 1.3 collective-permute-start.1
  14.1 5.0 collective-permute-start
  19.1 0.9 fusion.172
  20.0 0.9 fusion.171
  21.2 0.4 copy-done.11
  21.6 0.6 copy-done.13
  22.4 0.7 copy.73
  23.1 1.3 collective-permute-start.3
  24.4 0.7 copy.71
  25.2 4.7 collective-permute-start.2
  29.9 1.9 rev.26
  31.8 0.9 rev.25
  32.7 1.8 rev.24
  34.5 1.8 rev.23
  36.3 1.1 copy.74
  37.4 1.1 copy.72
  38.5 1.3 slice_select_fusion
  40.1 3.6 add_divide_fusion.1
  44.7 0.5 fusion.22
  45.2 0.9 copy-done.3
  46.1 14.5 %scatter_custom_fusion.1 = f32[4096]{0:T(1024)} fusion(s32[2048]{0:T(1024)S(1)} %pad_add_fusion, f32[2048]{0:T(1024)S(1)} %pad_maximum_fusion.9, f32[]{:T(128)} %constant.54.clone.1), kind=kCustom, calls=%fused_computation.342 | custom fusion | flops 2048 | bytes 16388 | tf_op jit(solution)/shard_map/scatter-add | solution.py:293
  60.6 0.6 eq.135
  61.6 0.7 reduce-window.12
  62.3 1.0 copy.95
  63.3 0.8 copy_bitcast_fusion.2
  64.1 0.9 maximum_bitcast_fusion
  65.1 2.7 copy.81
  67.8 0.9 slice_reduce_fusion
  68.7 1.1 compare_select_fusion
  69.8 21.7 %scatter_custom_fusion = bf16[12,256]{0,1:T(8,128)(2,1)} fusion(s32[8192]{0:T(1024)S(1)} %bitcast.214, bf16[8192,12]{1,0:T(8,128)(2,1)} %copy.81, bf16[]{:T(256)} %constant.78.clone.1), kind=kCustom, calls=%fused_computation.316 | custom fusion | bytes 6656 | tf_op jit(solution)/shard_map/scatter | solution.py:274
  91.5 3.2 fusion.16
  94.7 1.8 fusion.8
  96.7 24.0 %gather_fusion = bf16[8192,12]{1,0:T(8,128)(2,1)S(1)} fusion(bf16[12,256]{0,1:T(8,128)(2,1)S(1)} %copy.82, s32[8192]{0:T(1024)S(1)} %broadcast_clamp_fusion), kind=kCustom, calls=%fused_computation | custom fusion | bytes 425984 | tf_op jit(solution)/shard_map/gather | solution.py:277
  120.7 2.3 convert_element_type.31
  123.0 3.6 copy.84
  126.9 1.9 add_divide_fusion.2
  129.0 0.6 compare_bitcast_fusion.6
  129.6 0.7 add_multiply_fusion.8
  130.3 0.7 slice_exponential_fusion.8
  131.0 0.6 slice_exponential_fusion.10
  131.7 0.9 select_multiply_fusion.5
  132.6 1.1 slice_multiply_fusion.12
  134.0 2.0 fusion.169
  136.1 3.5 copy.79
  139.6 9.0 collective-permute-start.5
  148.6 2.1 copy.77
  150.7 2.1 collective-permute-start.4
  152.9 1.7 fusion.76
  154.6 1.1 slice.424
  155.7 0.6 copy.86
  156.6 1.1 slice.418
  157.6 0.6 copy.85
  158.7 3.9 add_divide_fusion
  163.6 0.6 fusion.24
  164.2 0.5 copy-done.4
  164.9 1.0 fusion.113
  165.9 721.4 %all-gather.3.cloned.1.call-done = f32[2097152]{0:T(1024)} async-done(((f32[4096]{0:T(1024)}), f32[2097152]{0:T(1024)}) %all-gather.3.cloned.1.call-update) | async-done | bytes 8388624 | tf_op jit(solution)/shard_map/all_gather | solution.py:294
  887.3 9.4 %reshape.288 = f32[512,4096]{1,0:T(8,128)} reshape(f32[2097152]{0:T(1024)} %all-gather.3.cloned.1.call-done) | data formatting | bytes 16777216 | tf_op jit(solution)/shard_map/all_gather | solution.py:294
  896.7 3.9 reduce_sum.100
  900.6 0.6 dynamic-slice_multiply_fusion
  (133 shorter events, 4.9 us)
Async XLA Ops:
  7.2 84.4 %copy-start = (bf16[800,1600]{1,0:T(8,128)(2,1)S(1)}, bf16[800,1600]{1,0:T(8,128)(2,1)}, u32[]{:S(2)}) copy-start(bf16[800,1600]{1,0:T(8,128)(2,1)} %param.11) | copy-start | bytes 7680004
  7.2 880.1 %all-gather.3.cloned.1.call-start = ((), (), s32[]{:S(2)}) async-start(), calls=%async_computation | async-start | bytes 8404992 | tf_op jit(solution)/shard_map/all_gather | solution.py:294
  12.7 8.2 copy-start.36
  12.8 8.2 copy-start.19
  12.8 8.2 copy-start.21
  12.8 8.1 collective-permute-start.1
  14.1 7.1 collective-permute-start
  20.9 0.7 copy-start.11
  21.6 0.7 copy-start.13
  23.1 13.2 %collective-permute-start.3 = (f32[12,14,3,128]{3,1,2,0:T(8,128)}, f32[12,14,3,128]{3,1,2,0:T(8,128)}, u32[]{:S(2)}, u32[]{:S(2)}) collective-permute-start(f32[12,14,3,128]{3,1,2,0:T(8,128)} %copy.73), channel_id=1, source_target_pairs={{4,0},{8,4},{12,8},{5,1},{9,5},{13,9},{6,2},{10,6},{14,10},{7,3},{... | collective-permute-start | bytes 774152 | tf_op jit(solution)/shard_map/ppermute | solution.py:23
  25.2 12.2 %collective-permute-start.2 = (f32[12,14,3,128]{3,1,2,0:T(8,128)}, f32[12,14,3,128]{3,1,2,0:T(8,128)}, u32[]{:S(2)}, u32[]{:S(2)}) collective-permute-start(f32[12,14,3,128]{3,1,2,0:T(8,128)} %copy.71), channel_id=1, source_target_pairs={{0,4},{4,8},{8,12},{1,5},{5,9},{9,13},{2,6},{6,10},{10,14},{3,7},{... | collective-permute-start | bytes 774152 | tf_op jit(solution)/shard_map/ppermute | solution.py:22
  38.5 1.3 copy-start.5
  44.7 15.9 %copy-start.34 = (s32[8,8,128]{2,1,0:T(8,128)S(1)}, s32[8,8,128]{2,1,0:T(8,128)}, u32[]{:S(2)}) copy-start(s32[8,8,128]{2,1,0:T(8,128)} %param.8) | copy-start | bytes 98308
  45.2 0.9 copy-start.3
  91.5 3.2 copy-start.37
  123.0 3.7 copy-start.12
  123.0 3.7 copy-start.14
  123.0 3.7 copy-start.20
  123.0 3.7 copy-start.22
  129.0 4.7 copy-start.23
  129.0 4.7 copy-start.25
  130.3 1.3 copy-start.31
  130.3 1.3 copy-start.33
  130.3 2.2 copy-start.27
  130.3 2.2 copy-start.29
  131.7 2.0 copy-start.6
  136.0 12.6 %copy-start.2 = (f32[12,14,14,3]{3,2,1,0:T(8,128)S(1)}, f32[12,14,14,3]{3,2,1,0:T(8,128)}, u32[]{:S(2)}) copy-start(f32[12,14,14,3]{3,2,1,0:T(8,128)} %get-tuple-element.60) | copy-start | bytes 84676
  136.0 16.8 %copy-start.15 = (f32[7,9,8,128]{3,2,1,0:T(8,128)S(1)}, f32[7,9,8,128]{3,2,1,0:T(8,128)}, u32[]{:S(2)}) copy-start(f32[7,9,8,128]{3,2,1,0:T(8,128)} %get-tuple-element.116) | copy-start | bytes 774148
  136.0 16.8 %copy-start.16 = (f32[7,9,8,128]{3,2,1,0:T(8,128)S(1)}, f32[7,9,8,128]{3,2,1,0:T(8,128)}, u32[]{:S(2)}) copy-start(f32[7,9,8,128]{3,2,1,0:T(8,128)} %get-tuple-element.117) | copy-start | bytes 774148
  136.0 16.8 %copy-start.17 = (f32[7,9,8,128]{3,2,1,0:T(8,128)S(1)}, f32[7,9,8,128]{3,2,1,0:T(8,128)}, u32[]{:S(2)}) copy-start(f32[7,9,8,128]{3,2,1,0:T(8,128)} %get-tuple-element.118) | copy-start | bytes 774148
  136.0 16.8 %copy-start.18 = (f32[7,9,8,128]{3,2,1,0:T(8,128)S(1)}, f32[7,9,8,128]{3,2,1,0:T(8,128)}, u32[]{:S(2)}) copy-start(f32[7,9,8,128]{3,2,1,0:T(8,128)} %get-tuple-element.174) | copy-start | bytes 774148
  136.0 16.8 %copy-start.24 = (f32[1,9,8,128]{3,2,1,0:T(8,128)S(1)}, f32[1,9,8,128]{3,2,1,0:T(8,128)}, u32[]{:S(2)}) copy-start(f32[1,9,8,128]{3,2,1,0:T(8,128)} %copy-done.23) | copy-start | bytes 110596
  136.0 16.8 %copy-start.26 = (f32[1,9,8,128]{3,2,1,0:T(8,128)S(1)}, f32[1,9,8,128]{3,2,1,0:T(8,128)}, u32[]{:S(2)}) copy-start(f32[1,9,8,128]{3,2,1,0:T(8,128)} %copy-done.25) | copy-start | bytes 110596
  136.0 16.8 %copy-start.28 = (f32[1,9,8,128]{3,2,1,0:T(8,128)S(1)}, f32[1,9,8,128]{3,2,1,0:T(8,128)}, u32[]{:S(2)}) copy-start(f32[1,9,8,128]{3,2,1,0:T(8,128)} %copy-done.27) | copy-start | bytes 110596
  136.0 16.8 %copy-start.30 = (f32[1,9,8,128]{3,2,1,0:T(8,128)S(1)}, f32[1,9,8,128]{3,2,1,0:T(8,128)}, u32[]{:S(2)}) copy-start(f32[1,9,8,128]{3,2,1,0:T(8,128)} %copy-done.29) | copy-start | bytes 110596
  136.1 16.8 %copy-start.32 = (f32[1,9,8,128]{3,2,1,0:T(8,128)S(1)}, f32[1,9,8,128]{3,2,1,0:T(8,128)}, u32[]{:S(2)}) copy-start(f32[1,9,8,128]{3,2,1,0:T(8,128)} %copy-done.31) | copy-start | bytes 110596
  136.1 16.8 %copy-start.35 = (pred[9,8,128]{2,1,0:T(8,128)(4,1)S(1)}, pred[9,8,128]{2,1,0:T(8,128)(4,1)}, u32[]{:S(2)}) copy-start(pred[9,8,128]{2,1,0:T(8,128)(4,1)} %compare_bitcast_fusion.6) | copy-start | bytes 27652
  139.6 15.0 %collective-permute-start.5 = (f32[12,14,14,3]{2,1,3,0:T(8,128)}, f32[12,14,14,3]{2,1,3,0:T(8,128)}, u32[]{:S(2)}, u32[]{:S(2)}) collective-permute-start(f32[12,14,14,3]{2,1,3,0:T(8,128)} %copy.79), channel_id=1, source_target_pairs={{1,0},{2,1},{3,2},{5,4},{6,5},{7,6},{9,8},{10,9},{11,10},{13,12},{... | collective-permute-start | bytes 84680 | tf_op jit(solution)/shard_map/ppermute | solution.py:23
  150.7 5.9 collective-permute-start.4
  152.9 5.3 copy-start.9
  152.9 5.3 copy-start.10
  163.6 1.1 copy-start.4
  163.6 1.2 copy-start.7
  163.6 1.3 copy-start.8
  896.7 4.5 copy-start.1
Sparse Core Ops, SparseCore 0:
  60.7 826.5 all-gather.2
